TPU v7x, 512 devices: a whole 4x4x16 slice. The times are simulated.
512 devices in a mesh: frame: 128 (over x, z, core), head: 4 (over y).
Axes of the slice: x: 4, y: 4, z: 16, core: 2. Of those that a mesh axis runs over, the one named last changes fastest.
Arguments:
- queries: bfloat16 [256, 384, 1024], P('frame', None, 'head'), may hold values from -12 to 12
- keys: bfloat16 [256, 384, 1024], P('frame', None, 'head'), may hold values from -5 to 5
- values: bfloat16 [256, 384, 1024], P('frame', None, 'head'), may hold values from -6 to 6
- pairs: int32 [256, 2], replicated, may hold values from 0 to 255, as said below
- out_weight: bfloat16 [1024, 1024], P('head'), may hold values from -0.1875 to 0.1875
Outputs:
- mixed: bfloat16 [256, 384, 1024], P('frame', None, 'head')
Inputs may be any that keep to these rules, and one draw needn't show every extreme that they name: `pairs`: each row (a, b) names two frames with a < b <= a + 2; no two rows name the same pair.
All inputs are finite; a program needn't handle non-finite values.
Results may differ from a plain program's by a relative error of at most 0.019.
Values may be sent and summed in bfloat16 or wider, within the bound.
A program may use at most 64 MiB of HBM per device.

v0:
```python
import jax
import jax.numpy as jnp
from jax import lax
from jax.sharding import PartitionSpec as P

HD = 64


def passed_along(x, axis, by):
    devices = lax.axis_size(axis)
    pairs = [(i, i + by) for i in range(devices) if 0 <= i + by < devices]
    return lax.ppermute(x, axis, pairs)


def attend(query, key_frame, value_frame):
    scores = (
        jnp.einsum("phd,khd->hpk", query, key_frame, preferred_element_type=jnp.float32) * 0.125
    )
    row_top = jnp.max(scores, axis=-1)
    weights = jnp.exp(scores - row_top[..., None]).astype(jnp.bfloat16)
    row_total = jnp.sum(weights, axis=-1, dtype=jnp.float32)
    summed = jnp.einsum("hpk,khd->phd", weights, value_frame, preferred_element_type=jnp.float32)
    partial_value = (summed / row_total.T[:, :, None]).astype(jnp.bfloat16)
    log_mass = (row_top + jnp.log(row_total)).T
    return (partial_value, log_mass)


def combine_states(states, partial_value, log_mass):
    peak_lse, weight_sum, weighted = states
    newest = jnp.maximum(peak_lse, log_mass)
    old_scale = jnp.exp(peak_lse - newest)
    new_scale = jnp.exp(log_mass - newest)
    return (
        newest,
        weight_sum * old_scale + new_scale,
        weighted * old_scale[..., None] + new_scale[..., None] * partial_value.astype(jnp.float32),
    )


def add_block(states, query_index, key_index, query_frames, key_frames, value_frames):
    partial_value, log_mass = attend(
        query_frames[query_index], key_frames[key_index], value_frames[key_index]
    )
    current = tuple((member[query_index] for member in states))
    merged = combine_states(current, partial_value, log_mass)
    return tuple((member.at[query_index].set(update) for member, update in zip(states, merged)))


def self_block(query, key_frame, value_frame):
    partial_value, log_mass = attend(query, key_frame, value_frame)
    return (log_mass, jnp.ones_like(log_mass), partial_value.astype(jnp.float32))


def body(queries, keys, values, pairs, out_weight):
    count_frames, tokens, feature_cols = queries.shape
    heads_here = feature_cols // HD
    framed = (count_frames, tokens, heads_here, HD)
    device_index = lax.axis_index("frame")
    own_first = device_index * count_frames
    query_frames = queries.reshape(framed)
    key_frames = keys.reshape(framed)
    value_frames = values.reshape(framed)
    states = jax.vmap(self_block)(query_frames, key_frames, value_frames)
    lower_end = pairs[:, 0]
    upper_end = pairs[:, 1]
    below_keys, below_values = passed_along((keys, values), "frame", 1)
    above_keys, above_values = passed_along((keys, values), "frame", -1)
    reach_shape = (3 * count_frames, tokens, heads_here, HD)
    key_reach = jnp.concatenate([below_keys, keys, above_keys], 0).reshape(reach_shape)
    value_reach = jnp.concatenate([below_values, values, above_values], 0).reshape(reach_shape)
    key_base = own_first - count_frames
    askers = jnp.concatenate([lower_end, upper_end])
    givers = jnp.concatenate([upper_end, lower_end])
    owned_mask = askers // count_frames == device_index
    event_order = jnp.argsort(jnp.where(owned_mask, 0, 1).astype(jnp.int32), stable=True)
    event_count = jnp.sum(owned_mask.astype(jnp.int32))

    def visit_event(position, states):
        event = event_order[position]
        return add_block(
            states,
            askers[event] - own_first,
            givers[event] - key_base,
            query_frames,
            key_reach,
            value_reach,
        )

    states = lax.fori_loop(0, event_count, visit_event, states)
    attention = (
        (states[2] / states[1][..., None])
        .astype(jnp.bfloat16)
        .reshape(count_frames * tokens, feature_cols)
    )
    term = jnp.dot(attention, out_weight, preferred_element_type=jnp.float32).reshape(
        count_frames, tokens, -1
    )
    return lax.psum_scatter(term.astype(jnp.bfloat16), "head", scatter_dimension=2, tiled=True)


def solution(mesh):
    placed = (
        P("frame", None, "head"),
        P("frame", None, "head"),
        P("frame", None, "head"),
        P(),
        P("head", None),
    )
    return jax.shard_map(
        body, mesh=mesh, in_specs=placed, out_specs=P("frame", None, "head"), check_vma=False
    )
```

profile of v0, /device:TPU:1, one launch (start us, length us, event | category | flops | bytes accessed | tf_op | source)
XLA Modules:
  0.0 181.2 jit_solution(17769156783857640712)
XLA Ops:
  6.5 8.9 %collective-permute-start.1 = (bf16[2,384,256]{2,1,0:T(8,128)(2,1)}, bf16[2,384,256]{2,1,0:T(8,128)(2,1)S(1)}, u32[]{:S(2)}, u32[]{:S(2)}) collective-permute-start(bf16[2,384,256]{2,1,0:T(8,128)(2,1)} %param.14), channel_id=1, source_target_pairs={{4,0},{8,4},{12,8},{16,12},{20,16},{24,20},{28,24},{32,28},{36,32}... | collective-permute-start | bytes 1179656 | tf_op jit(solution)/shard_map/ppermute | solution.py:12
  15.5 1.9 %collective-permute-start = (bf16[2,384,256]{2,1,0:T(8,128)(2,1)}, bf16[2,384,256]{2,1,0:T(8,128)(2,1)}, u32[]{:S(2)}, u32[]{:S(2)}) collective-permute-start(bf16[2,384,256]{2,1,0:T(8,128)(2,1)} %param.14), channel_id=1, source_target_pairs={{0,4},{4,8},{8,12},{12,16},{16,20},{20,24},{24,28},{28,32},{32,36}... | collective-permute-start | bytes 1179656 | tf_op jit(solution)/shard_map/ppermute | solution.py:12
  17.4 3.1 %collective-permute-start.3 = (bf16[2,384,256]{2,1,0:T(8,128)(2,1)}, bf16[2,384,256]{2,1,0:T(8,128)(2,1)}, u32[]{:S(2)}, u32[]{:S(2)}) collective-permute-start(bf16[2,384,256]{2,1,0:T(8,128)(2,1)} %param.15), channel_id=1, source_target_pairs={{4,0},{8,4},{12,8},{16,12},{20,16},{24,20},{28,24},{32,28},{36,32}... | collective-permute-start | bytes 1179656 | tf_op jit(solution)/shard_map/ppermute | solution.py:12
  20.5 2.4 %collective-permute-start.2 = (bf16[2,384,256]{2,1,0:T(8,128)(2,1)}, bf16[2,384,256]{2,1,0:T(8,128)(2,1)}, u32[]{:S(2)}, u32[]{:S(2)}) collective-permute-start(bf16[2,384,256]{2,1,0:T(8,128)(2,1)} %param.15), channel_id=1, source_target_pairs={{0,4},{4,8},{8,12},{12,16},{16,20},{20,24},{24,28},{28,32},{32,36}... | collective-permute-start | bytes 1179656 | tf_op jit(solution)/shard_map/ppermute | solution.py:12
  23.0 1.2 copy.16
  24.2 1.2 copy.17
  25.4 1.2 copy.15
  26.6 0.8 multiply_reduce_fusion.1
  27.5 0.8 convert_reduce_fusion.1
  28.3 1.0 fusion.26
  30.0 3.8 %sort.17 = (s32[512]{0:T(512)}, s32[512]{0:T(512)S(1)}) sort(s32[512]{0:T(512)S(1)} %get-tuple-element.144, s32[512]{0:T(512)S(1)} %iota.4), dimensions={0}, to_apply=%region_3.4 | sort | flops 4608 | bytes 8192 | tf_op jit(solution)/shard_map/jit(argsort)/sort | solution.py:75
  34.5 1.2 pad_maximum_fusion
  35.7 1.4 copy.19
  37.2 1.4 pad_maximum_fusion.1
  38.5 1.4 copy.20
  40.0 50.8 %while.17 = (s32[]{:T(128)}, f32[2,384,4]{1,2,0:T(4,128)S(1)}, f32[2,384,4]{1,2,0:T(4,128)S(1)}, f32[2,384,4,64]{1,3,2,0:T(8,128)S(1)}, s32[]{:T(128)}, /*index=...) while((s32[]{:T(128)}, f32[2,384,4]{1,2,0:T(4,128)S(1)}, ...), condition=%wide.region_9.10_spmd, body=%wide.region_4.9_spmd.sunk | while | flops 157593664 | bytes 9371601 | solution.py:89
  44.4 0.8 and_reduce_fusion.4
  46.3 1.5 multiply_reduce_fusion.3
  49.6 0.8 and_reduce_fusion.5
  50.4 2.2 %fusion.47 = f32[2,384,4,64]{1,3,2,0:T(8,128)S(1)} fusion(f32[2,384,4,64]{1,3,2,0:T(8,128)S(1)} %get-tuple-element.270, s32[]{:T(128)} %select_n.44, f32[1,384,4,64]{1,3,2,0:T(8,128)S(1)} %constant_dynamic-slice_fusion.7, f32[384,4]{0,1:T(4,128)S(1)} %bitcast.160, bf16[6,384,4,64]{1,3,2,0:T(8,128)(2,1)} %get-tuple-element.300, s32[]{:T(128)S(6)} %select_n.45, ...), kind=kOutput, calls=%fused_computation.11.clone.1 | convolution fusion | flops 77955072 | bytes 3367940 | tf_op jit(solution)/shard_map/while/body/hpk,khd->phd/dot_general | solution.py:22
  56.9 0.8 and_reduce_fusion.4
  58.9 1.5 multiply_reduce_fusion.3
  62.2 0.8 and_reduce_fusion.5
  63.0 2.2 %fusion.47 = f32[2,384,4,64]{1,3,2,0:T(8,128)S(1)} fusion(f32[2,384,4,64]{1,3,2,0:T(8,128)S(1)} %get-tuple-element.270, s32[]{:T(128)} %select_n.44, f32[1,384,4,64]{1,3,2,0:T(8,128)S(1)} %constant_dynamic-slice_fusion.7, f32[384,4]{0,1:T(4,128)S(1)} %bitcast.160, bf16[6,384,4,64]{1,3,2,0:T(8,128)(2,1)} %get-tuple-element.300, s32[]{:T(128)S(6)} %select_n.45, ...), kind=kOutput, calls=%fused_computation.11.clone.1 | convolution fusion | flops 77955072 | bytes 3367940 | tf_op jit(solution)/shard_map/while/body/hpk,khd->phd/dot_general | solution.py:22
  71.4 1.5 multiply_reduce_fusion.3
  74.7 0.8 and_reduce_fusion.5
  75.5 2.2 %fusion.47 = f32[2,384,4,64]{1,3,2,0:T(8,128)S(1)} fusion(f32[2,384,4,64]{1,3,2,0:T(8,128)S(1)} %get-tuple-element.270, s32[]{:T(128)} %select_n.44, f32[1,384,4,64]{1,3,2,0:T(8,128)S(1)} %constant_dynamic-slice_fusion.7, f32[384,4]{0,1:T(4,128)S(1)} %bitcast.160, bf16[6,384,4,64]{1,3,2,0:T(8,128)(2,1)} %get-tuple-element.300, s32[]{:T(128)S(6)} %select_n.45, ...), kind=kOutput, calls=%fused_computation.11.clone.1 | convolution fusion | flops 77955072 | bytes 3367940 | tf_op jit(solution)/shard_map/while/body/hpk,khd->phd/dot_general | solution.py:22
  84.0 1.5 multiply_reduce_fusion.3
  87.3 0.8 and_reduce_fusion.5
  88.1 2.2 %fusion.47 = f32[2,384,4,64]{1,3,2,0:T(8,128)S(1)} fusion(f32[2,384,4,64]{1,3,2,0:T(8,128)S(1)} %get-tuple-element.270, s32[]{:T(128)} %select_n.44, f32[1,384,4,64]{1,3,2,0:T(8,128)S(1)} %constant_dynamic-slice_fusion.7, f32[384,4]{0,1:T(4,128)S(1)} %bitcast.160, bf16[6,384,4,64]{1,3,2,0:T(8,128)(2,1)} %get-tuple-element.300, s32[]{:T(128)S(6)} %select_n.45, ...), kind=kOutput, calls=%fused_computation.11.clone.1 | convolution fusion | flops 77955072 | bytes 3367940 | tf_op jit(solution)/shard_map/while/body/hpk,khd->phd/dot_general | solution.py:22
  90.9 1.8 convolution_convert_fusion
  92.7 81.6 %reduce-scatter.2.cloned.1.call-done = bf16[2,384,256]{2,1,0:T(8,128)(2,1)} async-done(((bf16[2,384,1024]{2,1,0:T(8,128)(2,1)}), bf16[2,384,256]{2,1,0:T(8,128)(2,1)}) %reduce-scatter.2.cloned.1.call-update) | async-done | bytes 393232 | tf_op jit(solution)/shard_map/reduce_scatter | solution.py:98
  (59 shorter events, 17.4 us)
Async XLA Ops:
  6.5 84.4 %copy-start = (bf16[256,1024]{1,0:T(8,128)(2,1)S(1)}, bf16[256,1024]{1,0:T(8,128)(2,1)}, u32[]{:S(2)}) copy-start(bf16[256,1024]{1,0:T(8,128)(2,1)} %param.17) | copy-start | bytes 1572868
  6.5 20.1 %copy-start.5 = (s32[256,2]{0,1:T(2,128)S(1)}, s32[256,2]{0,1:T(2,128)}, u32[]{:S(2)}) copy-start(s32[256,2]{0,1:T(2,128)} %param.16) | copy-start | bytes 6148
  6.5 167.8 %reduce-scatter.2.cloned.1.call-start = ((), (), s32[]{:S(2)}) async-start(), calls=%async_computation.1 | async-start | bytes 1966080 | tf_op jit(solution)/shard_map/reduce_scatter | solution.py:98
  6.5 27.2 %collective-permute-start.1 = (bf16[2,384,256]{2,1,0:T(8,128)(2,1)}, bf16[2,384,256]{2,1,0:T(8,128)(2,1)S(1)}, u32[]{:S(2)}, u32[]{:S(2)}) collective-permute-start(bf16[2,384,256]{2,1,0:T(8,128)(2,1)} %param.14), channel_id=1, source_target_pairs={{4,0},{8,4},{12,8},{16,12},{20,16},{24,20},{28,24},{32,28},{36,32}... | collective-permute-start | bytes 1179656 | tf_op jit(solution)/shard_map/ppermute | solution.py:12
  15.5 19.0 %collective-permute-start = (bf16[2,384,256]{2,1,0:T(8,128)(2,1)}, bf16[2,384,256]{2,1,0:T(8,128)(2,1)}, u32[]{:S(2)}, u32[]{:S(2)}) collective-permute-start(bf16[2,384,256]{2,1,0:T(8,128)(2,1)} %param.14), channel_id=1, source_target_pairs={{0,4},{4,8},{8,12},{12,16},{16,20},{20,24},{24,28},{28,32},{32,36}... | collective-permute-start | bytes 1179656 | tf_op jit(solution)/shard_map/ppermute | solution.py:12
  17.4 19.8 %collective-permute-start.3 = (bf16[2,384,256]{2,1,0:T(8,128)(2,1)}, bf16[2,384,256]{2,1,0:T(8,128)(2,1)}, u32[]{:S(2)}, u32[]{:S(2)}) collective-permute-start(bf16[2,384,256]{2,1,0:T(8,128)(2,1)} %param.15), channel_id=1, source_target_pairs={{4,0},{8,4},{12,8},{16,12},{20,16},{24,20},{28,24},{32,28},{36,32}... | collective-permute-start | bytes 1179656 | tf_op jit(solution)/shard_map/ppermute | solution.py:12
  20.5 16.6 %collective-permute-start.2 = (bf16[2,384,256]{2,1,0:T(8,128)(2,1)}, bf16[2,384,256]{2,1,0:T(8,128)(2,1)}, u32[]{:S(2)}, u32[]{:S(2)}) collective-permute-start(bf16[2,384,256]{2,1,0:T(8,128)(2,1)} %param.15), channel_id=1, source_target_pairs={{0,4},{4,8},{8,12},{12,16},{16,20},{20,24},{24,28},{28,32},{32,36}... | collective-permute-start | bytes 1179656 | tf_op jit(solution)/shard_map/ppermute | solution.py:12
  28.3 6.2 %copy-start.1 = (bf16[2,384,256]{2,1,0:T(8,128)(2,1)S(1)}, bf16[2,384,256]{2,1,0:T(8,128)(2,1)}, u32[]{:S(2)}) copy-start(bf16[2,384,256]{2,1,0:T(8,128)(2,1)} %param.14) | copy-start | bytes 1179652
  33.7 0.7 copy-start.2
  37.2 2.8 %copy-start.3 = (s32[3]{0:T(128)S(1)}, s32[3]{0:T(128)}, u32[]{:S(2)}) copy-start(s32[3]{0:T(128)} %constant.95.clone.1) | copy-start | bytes 40
  37.2 2.8 %copy-start.4 = (s32[4]{0:T(128)S(1)}, s32[4]{0:T(128)}, u32[]{:S(2)}) copy-start(s32[4]{0:T(128)} %constant.101.clone.1) | copy-start | bytes 52
Sparse Core Ops, SparseCore 0:
  92.8 81.4 reduce-scatter.1
where the time goes:
time: 183 us; the launch traced here: 181 us
  waiting for transfers between devices  81.7 us (45%)
  other arithmetic  21.4 us (12%)
  matrix products  18.1 us (10%)
  starting transfers between devices  16.4 us (9%)
  loops' own time  15.7 us (9%)
  local copies, waits for them, and re-layouts  14.4 us (8%)
  between operations  13.6 us (7%)
    reduce_scatter x1, waiting for transfers between devices, body(): lax.psum_scatter(term.astype(jnp.bfloat16), 'head', scatter_dimension=2,...  81.6 us
    ppermute x4, starting transfers between devices, passed_along(): return lax.ppermute(x, axis, pairs)  16.4 us
    another operation x1, loops' own time, body(): states = lax.fori_loop(0, event_count, visit_event, states)  15.7 us
    dot_general x5, matrix products, attend(): jnp.einsum('hpk,khd->phd', weights, value_frame, preferred_element_type=j...  9.64 us
    dot_general x5, matrix products, attend(): jnp.einsum('phd,khd->hpk', query, key_frame, preferred_element_type=jnp.f...  6.68 us
    another operation x8, other arithmetic  6.26 us
    scatter x8, other arithmetic, add_block(): member.at[query_index].set(update)  5.57 us
    unnamed x15, local copies, waits for them, and re-layouts  4.39 us
  transfers between devices with their start and end apart: 5, of which 1 were waited for; matrix products, arithmetic and copies ran while one was open for 7% of the time, Pallas kernels for 0%

commit v1 on v0

v1 whole, which is shorter than its diff:
```python
import functools

import jax
import jax.numpy as jnp
from jax import lax
from jax.experimental import pallas as pl
from jax.experimental.pallas import tpu as pltpu
from jax.sharding import PartitionSpec as P

HD = 64
PAIR = 2 * HD
LOG2E = 1.4426950408889634
FAR = 1.0e5
MESH = pl.DeviceIdType.MESH
F32 = jnp.float32
BF16 = jnp.bfloat16
ACROSS = (((1,), (1,)), ((), ()))

PARTNER_FAR, PARTNER_NEAR, INNER, OUTER, NEXT_NEAR, NEXT_FAR = range(6)


def kernel(
    frames_axis,
    groups,
    q_hbm,
    k_hbm,
    v_hbm,
    pairs_ref,
    w_hbm,
    out_hbm,
    q_raw,
    q_cut,
    k_all,
    v_all,
    penalty,
    acc,
    top,
    gathered,
    w_all,
    mixed,
    send_sem,
    recv_sem,
    local_sem,
):
    tokens = q_hbm.shape[1]
    group_cols = q_hbm.shape[2]
    me = lax.axis_index("frame")
    group = lax.axis_index("head")
    core = lax.rem(me, 2)
    toward = 1 - 2 * core
    partner = me + toward
    beyond = lax.rem(me - toward + frames_axis, frames_axis)
    up = lax.rem(group + 1, groups)
    down = lax.rem(group + groups - 1, groups)
    across = lax.rem(group + 2, groups)
    outer = core
    inner = 1 - core

    barrier = pltpu.get_barrier_semaphore()
    for device in (
        (partner, group),
        (beyond, group),
        (me, up),
        (me, down),
        (me, across),
    ):
        pl.semaphore_signal(barrier, inc=1, device_id=device, device_id_type=MESH)

    def fetch(number, source, target):
        copy = pltpu.make_async_copy(source, target, local_sem.at[number])
        copy.start()
        return copy

    own_q = fetch(0, q_hbm, q_raw)
    own_kv = []
    for slot, frame in ((INNER, inner), (OUTER, outer)):
        for p in range(2):
            for which, (source, target) in enumerate(((k_hbm, k_all), (v_hbm, v_all))):
                own_kv.append(
                    fetch(
                        1 + len(own_kv),
                        source.at[frame, :, pl.ds(p * PAIR, PAIR)],
                        target.at[slot, p],
                    )
                )
    own_w = fetch(
        9, w_hbm.at[:, pl.ds(pl.multiple_of(group * group_cols, group_cols), group_cols)], w_all.at[0]
    )

    pl.semaphore_wait(barrier, 5)

    sends = []

    def send(source, target, device):
        number = len(sends)
        copy = pltpu.make_async_remote_copy(
            src_ref=source,
            dst_ref=target,
            send_sem=send_sem.at[number],
            recv_sem=recv_sem.at[number],
            device_id=device,
            device_id_type=MESH,
        )
        copy.start()
        sends.append(copy)
        return copy

    next_kv = {}
    for p in range(2):
        for slot, frame in ((NEXT_NEAR, outer), (NEXT_FAR, inner)):
            next_kv[slot, p] = [
                send(
                    source.at[frame, :, pl.ds(p * PAIR, PAIR)],
                    target.at[slot, p],
                    (beyond, group),
                )
                for source, target in ((k_hbm, k_all), (v_hbm, v_all))
            ]
    partner_kv = []
    for slot, frame in ((PARTNER_NEAR, inner), (PARTNER_FAR, outer)):
        for p in range(2):
            partner_kv += [
                send(
                    source.at[frame, :, pl.ds(p * PAIR, PAIR)],
                    target.at[slot, p],
                    (partner, group),
                )
                for source, target in ((k_hbm, k_all), (v_hbm, v_all))
            ]
    w_parts = [
        send(
            w_hbm.at[:, pl.ds(pl.multiple_of(there * group_cols, group_cols), group_cols)],
            w_all.at[place],
            (me, there),
        )
        for place, there in ((1, up), (2, down), (3, across))
    ]

    lower_end = pairs_ref[0:1, :]
    upper_end = pairs_ref[1:2, :]
    own_first = 2 * me

    def place_of(slot):
        steps = (3, 2, 1, 0, -1, -2)[slot]
        return own_first + outer + toward * steps

    for t, slot_q in enumerate((INNER, OUTER)):
        for slot in range(6):
            if slot == slot_q or abs(slot - slot_q) > 2:
                continue
            a, b = place_of(slot_q), place_of(slot)
            hit = (lower_end == jnp.minimum(a, b)) & (upper_end == jnp.maximum(a, b))
            missing = jnp.min(jnp.where(hit, 0.0, FAR).astype(F32), axis=1, keepdims=True)
            penalty[t, slot] = jnp.broadcast_to(missing, (8, PAIR))
        penalty[t, slot_q] = jnp.zeros((8, PAIR), F32)

    lane = lax.broadcasted_iota(jnp.int32, (tokens, PAIR), 1)
    first = lane < HD

    own_q.wait()
    for t, frame in enumerate((inner, outer)):
        for p in range(2):
            q = q_raw[frame, :, p * PAIR : (p + 1) * PAIR].astype(F32) * (0.125 * LOG2E)
            high = q.astype(BF16)
            low = (q - high.astype(F32)).astype(BF16)
            nothing = jnp.zeros_like(high)
            for h in range(2):
                mine = first if h == 0 else ~first
                q_cut[t, p, h, :, 0:PAIR] = jnp.where(mine, high, nothing)
                q_cut[t, p, h, :, PAIR : 2 * PAIR] = jnp.where(mine, low, nothing)

    def attend(t, p, h, low_slot, high_slot, old):
        count = high_slot - low_slot
        k = k_all[low_slot:high_slot, p].reshape(count * tokens, PAIR)
        v = v_all[low_slot:high_slot, p].reshape(count * tokens, PAIR)
        scores = lax.dot_general(
            q_cut[t, p, h], jnp.concatenate([k, k], 1), ACROSS, preferred_element_type=F32
        )
        highest = None
        for j in range(count):
            s = scores[:, j * tokens : (j + 1) * tokens]
            part = s[:, 0:PAIR]
            for c in range(1, tokens // PAIR):
                part = jnp.maximum(part, s[:, c * PAIR : (c + 1) * PAIR])
            part = part - penalty[t, low_slot + j, 0:1, :]
            highest = part if highest is None else jnp.maximum(highest, part)
        now = jnp.broadcast_to(jnp.max(highest, axis=1, keepdims=True), (tokens, PAIR))
        if old is not None:
            now = jnp.maximum(now, old[0])
        weights = []
        for j in range(count):
            less = now + penalty[t, low_slot + j, 0:1, :]
            for c in range(tokens // PAIR):
                at = j * tokens + c * PAIR
                weights.append(jnp.exp2((scores[:, at : at + PAIR] - less).astype(BF16)))
        summed = jnp.dot(
            jnp.concatenate(weights, 1),
            jnp.concatenate([v, jnp.ones_like(v)], 1),
            preferred_element_type=F32,
        )
        if old is not None:
            scale = jnp.exp2(old[0] - now)
            summed = summed + old[1] * jnp.concatenate([scale, scale], 1)
        return now, summed

    for copy in own_kv:
        copy.wait()
    for copy in partner_kv:
        copy.wait_recv()

    def near_frames(p, carry):
        for t, low_slot, high_slot in ((0, 0, 4), (1, 1, 4)):
            for h in range(2):
                now, summed = attend(t, p, h, low_slot, high_slot, None)
                top[t, p, h] = now
                acc[t, p, h] = summed
        return carry

    lax.fori_loop(0, 2, near_frames, 0)

    def finish(t, p, results):
        parts = [summed[:, 0:PAIR] / summed[:, PAIR : 2 * PAIR] for _, summed in results]
        gathered[0, t, p] = jnp.where(first, parts[0], parts[1]).astype(BF16)
        return [
            send(gathered.at[0, t, p], gathered.at[1, t, p], (me, up)),
            send(gathered.at[0, t, p], gathered.at[2, t, p], (me, down)),
        ]

    half = tokens // 2

    def pass_on(t, p, direct):
        for copy in direct:
            copy.wait_recv()
        return [
            send(
                gathered.at[1, t, p, pl.ds(0, half)],
                gathered.at[3, t, p, pl.ds(0, half)],
                (me, up),
            ),
            send(
                gathered.at[2, t, p, pl.ds(half, half)],
                gathered.at[3, t, p, pl.ds(half, half)],
                (me, down),
            ),
        ]

    def project(t, p, source):
        return jnp.dot(
            gathered[source, t, p],
            w_all[source, p * PAIR : (p + 1) * PAIR, :],
            preferred_element_type=F32,
        )

    def project_both(t, source):
        return jnp.dot(
            jnp.concatenate([gathered[source, t, 0], gathered[source, t, 1]], 1),
            w_all[source],
            preferred_element_type=F32,
        )

    def write(t, frame, total):
        mixed[t] = total.astype(BF16)
        return fetch(10 + t, mixed.at[t], out_hbm.at[frame])

    direct, forward = {}, {}
    for p in range(2):
        for copy in next_kv[NEXT_NEAR, p]:
            copy.wait_recv()
        results = [
            attend(0, p, h, NEXT_NEAR, NEXT_NEAR + 1, (top[0, p, h], acc[0, p, h])) for h in range(2)
        ]
        direct[0, p] = finish(0, p, results)
        for h in range(2):
            now, summed = attend(1, p, h, NEXT_NEAR, NEXT_NEAR + 1, (top[1, p, h], acc[1, p, h]))
            top[1, p, h] = now
            acc[1, p, h] = summed
        if p == 1:
            forward[1, 0] = pass_on(1, 0, direct[1, 0])
        for copy in next_kv[NEXT_FAR, p]:
            copy.wait_recv()
        results = [
            attend(1, p, h, NEXT_FAR, NEXT_FAR + 1, (top[1, p, h], acc[1, p, h])) for h in range(2)
        ]
        direct[1, p] = finish(1, p, results)
        forward[0, p] = pass_on(0, p, direct[0, p])

    own_w.wait()
    for copy in w_parts + forward[0, 0] + forward[1, 0]:
        copy.wait_recv()
    total = project(1, 0, 0)
    for source in range(1, 4):
        total = total + project(1, 0, source)
    total = total + project(1, 1, 0)
    forward[1, 1] = pass_on(1, 1, direct[1, 1])
    total = total + project(1, 1, 1) + project(1, 1, 2)
    for copy in forward[0, 1]:
        copy.wait_recv()
    other = project_both(0, 0)
    for source in range(1, 4):
        other = other + project_both(0, source)
    out_inner = write(0, inner, other)
    for copy in forward[1, 1]:
        copy.wait_recv()
    out_outer = write(1, outer, total + project(1, 1, 3))
    for copy in sends:
        copy.wait_send()
    out_inner.wait()
    out_outer.wait()


def body(queries, keys, values, pairs, out_weight):
    own_frames, tokens, cols = queries.shape
    frames_axis = lax.axis_size("frame")
    groups = lax.axis_size("head")
    assert own_frames == 2 and cols == 4 * HD and groups == 4
    anywhere = pl.BlockSpec(memory_space=pl.ANY)
    in_place = pl.BlockSpec(memory_space=pltpu.HBM)
    multiply_adds = 10 * 4 * tokens * tokens * (4 * HD + 4 * HD) + 2 * tokens * groups * cols * cols
    return pl.pallas_call(
        functools.partial(kernel, frames_axis, groups),
        out_shape=jax.ShapeDtypeStruct(queries.shape, BF16),
        in_specs=[in_place] * 3 + [pl.BlockSpec(memory_space=pltpu.VMEM), in_place],
        out_specs=anywhere,
        scratch_shapes=[
            pltpu.VMEM((2, tokens, cols), BF16),
            pltpu.VMEM((2, 2, 2, tokens, 2 * PAIR), BF16),
            pltpu.VMEM((6, 2, tokens, PAIR), BF16),
            pltpu.VMEM((6, 2, tokens, PAIR), BF16),
            pltpu.VMEM((2, 6, 8, PAIR), F32),
            pltpu.VMEM((2, 2, 2, tokens, 2 * PAIR), F32),
            pltpu.VMEM((2, 2, 2, tokens, PAIR), F32),
            pltpu.VMEM((4, 2, 2, tokens, PAIR), BF16),
            pltpu.VMEM((4, cols, cols), BF16),
            pltpu.VMEM((2, tokens, cols), BF16),
            pltpu.SemaphoreType.DMA((35,)),
            pltpu.SemaphoreType.DMA((35,)),
            pltpu.SemaphoreType.DMA((12,)),
        ],
        compiler_params=pltpu.CompilerParams(
            collective_id=0, has_side_effects=True, vmem_limit_bytes=48 * 2**20
        ),
        cost_estimate=pl.CostEstimate(
            flops=2 * multiply_adds, bytes_accessed=4 * queries.size * 2, transcendentals=0
        ),
    )(queries, keys, values, pairs.T, out_weight)


def solution(mesh):
    placed = (
        P("frame", None, "head"),
        P("frame", None, "head"),
        P("frame", None, "head"),
        P(),
        P("head", None),
    )
    return jax.shard_map(
        body, mesh=mesh, in_specs=placed, out_specs=P("frame", None, "head"), check_vma=False
    )
```

time: 183 us -> 47 us (0.26)
  waiting for transfers between devices: 81.7 us -> 0 us
  Pallas kernels: 0 us -> 41.2 us
  other arithmetic: 21.4 us -> 0 us
  matrix products: 18.1 us -> 0 us
  starting transfers between devices: 16.4 us -> 0 us
  loops' own time: 15.7 us -> 0 us
  between operations: 13.6 us -> 0.01 us
  local copies, waits for them, and re-layouts: 14.4 us -> 5.46 us
    reduce_scatter x1 -> x0, waiting for transfers between devices: 81.6 us -> none  [body(): lax.psum_scatter(term.astype(jnp.bfloat16), 'head', scatter_dimension=2,...]
    pallas_call x0 -> x1, Pallas kernels: none -> 41.2 us  [body(): pl.pallas_call(functools.partial(kernel, frames_axis, groups), out_shape=...]
    dot_general x11 -> x0, matrix products: 18.1 us -> none  [the longest x5 9.64 us: attend(): jnp.einsum('hpk,khd->phd', weights, value_frame, preferred_element_type=j...]
    ppermute x4 -> x0, starting transfers between devices: 16.4 us -> none  [passed_along(): return lax.ppermute(x, axis, pairs)]
    another operation x1 -> x0, loops' own time: 15.7 us -> none  [body(): states = lax.fori_loop(0, event_count, visit_event, states)]
    dynamic_slice x20 -> x0, local copies, waits for them, and re-layouts: 7.15 us -> none  [the longest x4 2.35 us: visit_event(): event = event_order[position]]
    another operation x8 -> x0, other arithmetic: 6.26 us -> none
    scatter x8 -> x0, other arithmetic: 5.57 us -> none  [add_block(): member.at[query_index].set(update)]
  transfers between devices with their start and end apart: 5 -> 0, of which waited for: 1 -> 0; matrix products, arithmetic and copies ran while one was open for 7% -> 0% of each run, Pallas kernels for 0% -> 0%
where the time goes in v1:
time: 47 us; the launch traced here: 46.7 us
  Pallas kernels  41.2 us (88%)
  local copies, waits for them, and re-layouts  5.46 us (12%)
    pallas_call x1, Pallas kernels, body(): pl.pallas_call(functools.partial(kernel, frames_axis, groups), out_shape=...  41.2 us
    unnamed x11, local copies, waits for them, and re-layouts  5.46 us

profile of v1, /device:TPU:1, one launch (start us, length us, event | category | flops | bytes accessed | tf_op | source)
XLA Modules:
  0.0 46.7 jit_solution(2848574264956983109)
XLA Ops:
  0.0 0.0 copy-start
  0.0 1.0 %copy-done = bf16[256,1024]{1,0:T(8,128)(2,1)S(1)} copy-done((bf16[256,1024]{1,0:T(8,128)(2,1)S(1)}, bf16[256,1024]{1,0:T(8,128)(2,1)}, u32[]{:S(2)}) %copy-start) | copy-done | bytes 524312
  1.0 0.0 copy-start.1
  1.0 1.0 %copy-done.1 = bf16[2,384,256]{2,1,0:T(8,128)(2,1)S(1)} copy-done((bf16[2,384,256]{2,1,0:T(8,128)(2,1)S(1)}, bf16[2,384,256]{2,1,0:T(8,128)(2,1)}, u32[]{:S(2)}) %copy-start.1) | copy-done | bytes 393240
  2.0 0.0 copy-start.2
  2.0 1.0 %copy-done.2 = bf16[2,384,256]{2,1,0:T(8,128)(2,1)S(1)} copy-done((bf16[2,384,256]{2,1,0:T(8,128)(2,1)S(1)}, bf16[2,384,256]{2,1,0:T(8,128)(2,1)}, u32[]{:S(2)}) %copy-start.2) | copy-done | bytes 393240
  3.0 0.0 copy-start.3
  3.0 1.0 %copy-done.3 = bf16[2,384,256]{2,1,0:T(8,128)(2,1)S(1)} copy-done((bf16[2,384,256]{2,1,0:T(8,128)(2,1)S(1)}, bf16[2,384,256]{2,1,0:T(8,128)(2,1)}, u32[]{:S(2)}) %copy-start.3) | copy-done | bytes 393240
  4.0 0.0 copy-start.4
  4.0 0.7 %copy-done.4 = s32[256,2]{0,1:T(2,128)S(1)} copy-done((s32[256,2]{0,1:T(2,128)S(1)}, s32[256,2]{0,1:T(2,128)}, u32[]{:S(2)}) %copy-start.4) | copy-done | bytes 2072
  4.7 41.2 %shard_map.55 = bf16[2,384,256]{2,1,0:T(8,128)(2,1)S(1)} custom-call(bf16[2,384,256]{2,1,0:T(8,128)(2,1)S(1)} %copy-done.1, bf16[2,384,256]{2,1,0:T(8,128)(2,1)S(1)} %copy-done.2, bf16[2,384,256]{2,1,0:T(8,128)(2,1)S(1)} %copy-done.3, s32[2,256]{1,0:T(2,128)S(1)} %bitcast.1, bf16[256,1024]{1,0:T(8,128)(2,1)S(1)} %copy-done), custom_call_target="tpu_custom_call" | custom-call | flops 6442450944 | bytes 1572864 | tf_op jit(solution)/shard_map/pallas_call | solution.py:319
  46.0 0.7 %copy.7 = bf16[2,384,256]{2,1,0:T(8,128)(2,1)} copy(bf16[2,384,256]{2,1,0:T(8,128)(2,1)S(1)} %shard_map.55) | data formatting | bytes 786432
Async XLA Ops:
  0.0 1.0 %copy-start = (bf16[256,1024]{1,0:T(8,128)(2,1)S(1)}, bf16[256,1024]{1,0:T(8,128)(2,1)}, u32[]{:S(2)}) copy-start(bf16[256,1024]{1,0:T(8,128)(2,1)} %w_hbm.1) | copy-start | bytes 1572868
  1.0 1.0 %copy-start.1 = (bf16[2,384,256]{2,1,0:T(8,128)(2,1)S(1)}, bf16[2,384,256]{2,1,0:T(8,128)(2,1)}, u32[]{:S(2)}) copy-start(bf16[2,384,256]{2,1,0:T(8,128)(2,1)} %q_hbm.1) | copy-start | bytes 1179652
  2.0 1.0 %copy-start.2 = (bf16[2,384,256]{2,1,0:T(8,128)(2,1)S(1)}, bf16[2,384,256]{2,1,0:T(8,128)(2,1)}, u32[]{:S(2)}) copy-start(bf16[2,384,256]{2,1,0:T(8,128)(2,1)} %k_hbm.1) | copy-start | bytes 1179652
  3.0 1.0 %copy-start.3 = (bf16[2,384,256]{2,1,0:T(8,128)(2,1)S(1)}, bf16[2,384,256]{2,1,0:T(8,128)(2,1)}, u32[]{:S(2)}) copy-start(bf16[2,384,256]{2,1,0:T(8,128)(2,1)} %v_hbm.1) | copy-start | bytes 1179652
  4.0 0.7 %copy-start.4 = (s32[256,2]{0,1:T(2,128)S(1)}, s32[256,2]{0,1:T(2,128)}, u32[]{:S(2)}) copy-start(s32[256,2]{0,1:T(2,128)} %param.8) | copy-start | bytes 6148

commit v2 on v1

--- a/solution.py
+++ b/solution.py
@@ -11,6 +11,7 @@
 PAIR = 2 * HD
 LOG2E = 1.4426950408889634
 FAR = 1.0e5
+RUN = 32
 MESH = pl.DeviceIdType.MESH
 F32 = jnp.float32
 BF16 = jnp.bfloat16
@@ -27,7 +28,7 @@
     v_hbm,
     pairs_ref,
     w_hbm,
-    out_hbm,
+    mixed,
     q_raw,
     q_cut,
     k_all,
@@ -37,10 +38,10 @@
     top,
     gathered,
     w_all,
-    mixed,
     send_sem,
     recv_sem,
     local_sem,
+    ready,
 ):
     tokens = q_hbm.shape[1]
     group_cols = q_hbm.shape[2]
@@ -55,16 +56,15 @@
     across = lax.rem(group + 2, groups)
     outer = core
     inner = 1 - core
+    late = lax.rem(me, RUN) == 0
 
     barrier = pltpu.get_barrier_semaphore()
-    for device in (
-        (partner, group),
-        (beyond, group),
-        (me, up),
-        (me, down),
-        (me, across),
-    ):
+    for device in ((partner, group), (me, up), (me, down), (me, across)):
         pl.semaphore_signal(barrier, inc=1, device_id=device, device_id_type=MESH)
+
+    @pl.when(core == 0)
+    def _():
+        pl.semaphore_signal(barrier, inc=1, device_id=(beyond, group), device_id_type=MESH)
 
     def fetch(number, source, target):
         copy = pltpu.make_async_copy(source, target, local_sem.at[number])
@@ -87,11 +87,12 @@
         9, w_hbm.at[:, pl.ds(pl.multiple_of(group * group_cols, group_cols), group_cols)], w_all.at[0]
     )
 
-    pl.semaphore_wait(barrier, 5)
+    pl.semaphore_wait(barrier, 4 + core)
+
 
     sends = []
 
-    def send(source, target, device):
+    def prepare(source, target, device):
         number = len(sends)
         copy = pltpu.make_async_remote_copy(
             src_ref=source,
@@ -101,21 +102,33 @@
             device_id=device,
             device_id_type=MESH,
         )
+        sends.append(copy)
+        return copy
+
+    def send(source, target, device):
+        copy = prepare(source, target, device)
         copy.start()
-        sends.append(copy)
         return copy
 
     next_kv = {}
     for p in range(2):
         for slot, frame in ((NEXT_NEAR, outer), (NEXT_FAR, inner)):
             next_kv[slot, p] = [
-                send(
+                prepare(
                     source.at[frame, :, pl.ds(p * PAIR, PAIR)],
                     target.at[slot, p],
                     (beyond, group),
                 )
                 for source, target in ((k_hbm, k_all), (v_hbm, v_all))
             ]
+
+    @pl.when(core == 1)
+    def _():
+        pl.semaphore_signal(ready, inc=1, device_id=(beyond, group), device_id_type=MESH)
+        for copies in next_kv.values():
+            for copy in copies:
+                copy.start()
+
     partner_kv = []
     for slot, frame in ((PARTNER_NEAR, inner), (PARTNER_FAR, outer)):
         for p in range(2):
@@ -127,10 +140,11 @@
                 )
                 for source, target in ((k_hbm, k_all), (v_hbm, v_all))
             ]
+    rows = pl.ds(pl.multiple_of(core * (group_cols // 2), group_cols // 2), group_cols // 2)
     w_parts = [
         send(
-            w_hbm.at[:, pl.ds(pl.multiple_of(there * group_cols, group_cols), group_cols)],
-            w_all.at[place],
+            w_hbm.at[rows, pl.ds(pl.multiple_of(there * group_cols, group_cols), group_cols)],
+            w_all.at[place, rows],
             (me, there),
         )
         for place, there in ((1, up), (2, down), (3, across))
@@ -203,28 +217,33 @@
             summed = summed + old[1] * jnp.concatenate([scale, scale], 1)
         return now, summed
 
+    def start_beyond():
+        pl.semaphore_wait(ready, 1)
+        for copies in next_kv.values():
+            for copy in copies:
+                copy.start()
+
+    @pl.when((core == 0) & ~late)
+    def _():
+        start_beyond()
+
     for copy in own_kv:
         copy.wait()
     for copy in partner_kv:
         copy.wait_recv()
 
-    def near_frames(p, carry):
+    def near_frames(p):
         for t, low_slot, high_slot in ((0, 0, 4), (1, 1, 4)):
             for h in range(2):
                 now, summed = attend(t, p, h, low_slot, high_slot, None)
                 top[t, p, h] = now
                 acc[t, p, h] = summed
-        return carry
-
-    lax.fori_loop(0, 2, near_frames, 0)
 
     def finish(t, p, results):
         parts = [summed[:, 0:PAIR] / summed[:, PAIR : 2 * PAIR] for _, summed in results]
         gathered[0, t, p] = jnp.where(first, parts[0], parts[1]).astype(BF16)
-        return [
-            send(gathered.at[0, t, p], gathered.at[1, t, p], (me, up)),
-            send(gathered.at[0, t, p], gathered.at[2, t, p], (me, down)),
-        ]
+        targets = [(1, up), (2, down)] + ([(3, across)] if (t, p) == (1, 1) else [])
+        return [send(gathered.at[0, t, p], gathered.at[place, t, p], (me, there)) for place, there in targets]
 
     half = tokens // 2
 
@@ -244,26 +263,29 @@
             ),
         ]
 
-    def project(t, p, source):
+    def project(t, *parts):
         return jnp.dot(
-            gathered[source, t, p],
-            w_all[source, p * PAIR : (p + 1) * PAIR, :],
+            jnp.concatenate([gathered[source, t, p] for source, p in parts], 1),
+            jnp.concatenate([w_all[source, p * PAIR : (p + 1) * PAIR, :] for source, p in parts], 0),
             preferred_element_type=F32,
         )
-
-    def project_both(t, source):
-        return jnp.dot(
-            jnp.concatenate([gathered[source, t, 0], gathered[source, t, 1]], 1),
-            w_all[source],
-            preferred_element_type=F32,
-        )
-
-    def write(t, frame, total):
-        mixed[t] = total.astype(BF16)
-        return fetch(10 + t, mixed.at[t], out_hbm.at[frame])
 
     direct, forward = {}, {}
     for p in range(2):
+        if p == 0:
+            near_frames(0)
+
+            @pl.when(late)
+            def _():
+                near_frames(1)
+                start_beyond()
+
+        else:
+
+            @pl.when(~late)
+            def _():
+                near_frames(1)
+
         for copy in next_kv[NEXT_NEAR, p]:
             copy.wait_recv()
         results = [
@@ -283,29 +305,24 @@
         ]
         direct[1, p] = finish(1, p, results)
         forward[0, p] = pass_on(0, p, direct[0, p])
+        if p == 0:
+            for copy in w_parts:
+                copy.wait_recv()
+            w_shared = send(w_all.at[pl.ds(1, 3), rows], w_all.at[pl.ds(1, 3), rows], (partner, group))
 
     own_w.wait()
-    for copy in w_parts + forward[0, 0] + forward[1, 0]:
+    for copy in [w_shared] + forward[0, 0] + forward[1, 0]:
         copy.wait_recv()
-    total = project(1, 0, 0)
-    for source in range(1, 4):
-        total = total + project(1, 0, source)
-    total = total + project(1, 1, 0)
-    forward[1, 1] = pass_on(1, 1, direct[1, 1])
-    total = total + project(1, 1, 1) + project(1, 1, 2)
+    total = project(1, (0, 0), (0, 1), (1, 0), (2, 0), (3, 0))
+    other = project(0, (0, 0), (0, 1), (1, 0), (1, 1), (2, 0), (2, 1), (3, 0))
     for copy in forward[0, 1]:
         copy.wait_recv()
-    other = project_both(0, 0)
-    for source in range(1, 4):
-        other = other + project_both(0, source)
-    out_inner = write(0, inner, other)
-    for copy in forward[1, 1]:
+    mixed[inner] = (other + project(0, (3, 1))).astype(BF16)
+    for copy in direct[1, 1]:
         copy.wait_recv()
-    out_outer = write(1, outer, total + project(1, 1, 3))
+    mixed[outer] = (total + project(1, (1, 1), (2, 1), (3, 1))).astype(BF16)
     for copy in sends:
         copy.wait_send()
-    out_inner.wait()
-    out_outer.wait()
 
 
 def body(queries, keys, values, pairs, out_weight):
@@ -313,14 +330,13 @@
     frames_axis = lax.axis_size("frame")
     groups = lax.axis_size("head")
     assert own_frames == 2 and cols == 4 * HD and groups == 4
-    anywhere = pl.BlockSpec(memory_space=pl.ANY)
     in_place = pl.BlockSpec(memory_space=pltpu.HBM)
     multiply_adds = 10 * 4 * tokens * tokens * (4 * HD + 4 * HD) + 2 * tokens * groups * cols * cols
     return pl.pallas_call(
         functools.partial(kernel, frames_axis, groups),
         out_shape=jax.ShapeDtypeStruct(queries.shape, BF16),
         in_specs=[in_place] * 3 + [pl.BlockSpec(memory_space=pltpu.VMEM), in_place],
-        out_specs=anywhere,
+        out_specs=pl.BlockSpec(memory_space=pltpu.VMEM),
         scratch_shapes=[
             pltpu.VMEM((2, tokens, cols), BF16),
             pltpu.VMEM((2, 2, 2, tokens, 2 * PAIR), BF16),
@@ -331,13 +347,13 @@
             pltpu.VMEM((2, 2, 2, tokens, PAIR), F32),
             pltpu.VMEM((4, 2, 2, tokens, PAIR), BF16),
             pltpu.VMEM((4, cols, cols), BF16),
-            pltpu.VMEM((2, tokens, cols), BF16),
             pltpu.SemaphoreType.DMA((35,)),
             pltpu.SemaphoreType.DMA((35,)),
-            pltpu.SemaphoreType.DMA((12,)),
+            pltpu.SemaphoreType.DMA((10,)),
+            pltpu.SemaphoreType.REGULAR,
         ],
         compiler_params=pltpu.CompilerParams(
-            collective_id=0, has_side_effects=True, vmem_limit_bytes=48 * 2**20
+            collective_id=0, has_side_effects=True, vmem_limit_bytes=62 * 2**20
         ),
         cost_estimate=pl.CostEstimate(
             flops=2 * multiply_adds, bytes_accessed=4 * queries.size * 2, transcendentals=0

time: 47 us -> 38.8 us (0.83)
  Pallas kernels: 41.2 us -> 36.7 us
  local copies, waits for them, and re-layouts: 5.46 us -> 1.77 us
    pallas_call x1, Pallas kernels: 41.2 us -> 36.7 us  [body(): pl.pallas_call(functools.partial(kernel, frames_axis, groups), out_shape=...]
    unnamed x11 -> x1, local copies, waits for them, and re-layouts: 5.46 us -> 1.77 us
where the time goes in v2:
time: 38.8 us; the launch traced here: 38.5 us
  Pallas kernels  36.7 us (95%)
  local copies, waits for them, and re-layouts  1.77 us (5%)
    pallas_call x1, Pallas kernels, body(): pl.pallas_call(functools.partial(kernel, frames_axis, groups), out_shape=...  36.7 us
    unnamed x1, local copies, waits for them, and re-layouts  1.77 us

profile of v2, /device:TPU:1, one launch (start us, length us, event | category | flops | bytes accessed | tf_op | source)
XLA Modules:
  0.0 38.5 jit_solution(16393935922313033063)
XLA Ops:
  0.0 36.7 %shard_map.55 = bf16[2,384,256]{2,1,0:T(8,128)(2,1)} custom-call(bf16[2,384,256]{2,1,0:T(8,128)(2,1)} %q_hbm.1, bf16[2,384,256]{2,1,0:T(8,128)(2,1)} %k_hbm.1, bf16[2,384,256]{2,1,0:T(8,128)(2,1)} %v_hbm.1, s32[2,256]{1,0:T(2,128)} %bitcast.1, bf16[256,1024]{1,0:T(8,128)(2,1)} %w_hbm.1), custom_call_target="tpu_custom_call" | custom-call | flops 6442450944 | bytes 1572864 | tf_op jit(solution)/shard_map/pallas_call | solution.py:335
  36.7 1.8 %copy.7 = bf16[2,384,256]{2,1,0:T(8,128)(2,1)} copy(bf16[2,384,256]{2,1,0:T(8,128)(2,1)} %shard_map.55) | data formatting | bytes 786432

commit v3 on v2

--- a/solution.py
+++ b/solution.py
@@ -11,6 +11,7 @@
 PAIR = 2 * HD
 LOG2E = 1.4426950408889634
 FAR = 1.0e5
+GRANT = 107 * 2**19
 RUN = 32
 MESH = pl.DeviceIdType.MESH
 F32 = jnp.float32
@@ -26,9 +27,10 @@
     q_hbm,
     k_hbm,
     v_hbm,
-    pairs_ref,
+    pairs_hbm,
     w_hbm,
     mixed,
+    pairs_ref,
     q_raw,
     q_cut,
     k_all,
@@ -71,6 +73,7 @@
         copy.start()
         return copy
 
+    own_pairs = fetch(10, pairs_hbm, pairs_ref)
     own_q = fetch(0, q_hbm, q_raw)
     own_kv = []
     for slot, frame in ((INNER, inner), (OUTER, outer)):
@@ -150,6 +153,7 @@
         for place, there in ((1, up), (2, down), (3, across))
     ]
 
+    own_pairs.wait()
     lower_end = pairs_ref[0:1, :]
     upper_end = pairs_ref[1:2, :]
     own_first = 2 * me
@@ -229,39 +233,68 @@
 
     for copy in own_kv:
         copy.wait()
-    for copy in partner_kv:
-        copy.wait_recv()
-
-    def near_frames(p):
-        for t, low_slot, high_slot in ((0, 0, 4), (1, 1, 4)):
+
+    def visit(p, reach, merge):
+        for t, (low_slot, high_slot) in enumerate(reach):
             for h in range(2):
-                now, summed = attend(t, p, h, low_slot, high_slot, None)
+                old = (top[t, p, h], acc[t, p, h]) if merge else None
+                now, summed = attend(t, p, h, low_slot, high_slot, old)
                 top[t, p, h] = now
                 acc[t, p, h] = summed
+
+    def near_frames(p):
+        visit(p, ((PARTNER_FAR, NEXT_NEAR), (PARTNER_NEAR, NEXT_NEAR)), False)
+
+    direct, forward, only_late = {}, {}, []
 
     def finish(t, p, results):
         parts = [summed[:, 0:PAIR] / summed[:, PAIR : 2 * PAIR] for _, summed in results]
         gathered[0, t, p] = jnp.where(first, parts[0], parts[1]).astype(BF16)
-        targets = [(1, up), (2, down)] + ([(3, across)] if (t, p) == (1, 1) else [])
-        return [send(gathered.at[0, t, p], gathered.at[place, t, p], (me, there)) for place, there in targets]
+        direct[t, p] = [
+            send(gathered.at[0, t, p], gathered.at[place, t, p], (me, there))
+            for place, there in ((1, up), (2, down))
+        ]
+        whole = prepare(gathered.at[0, t, p], gathered.at[3, t, p], (me, across))
+        if (t, p) == (1, 1):
+            whole.start()
+        else:
+            pl.when(late)(whole.start)
+            only_late.append(whole)
+        direct[t, p].append(whole)
 
     half = tokens // 2
 
-    def pass_on(t, p, direct):
-        for copy in direct:
-            copy.wait_recv()
-        return [
-            send(
+    def pass_on(t, p):
+        forward[t, p] = [
+            prepare(
                 gathered.at[1, t, p, pl.ds(0, half)],
                 gathered.at[3, t, p, pl.ds(0, half)],
                 (me, up),
             ),
-            send(
+            prepare(
                 gathered.at[2, t, p, pl.ds(half, half)],
                 gathered.at[3, t, p, pl.ds(half, half)],
                 (me, down),
             ),
         ]
+
+        @pl.when(~late)
+        def _():
+            for copy in direct[t, p][:2]:
+                copy.wait_recv()
+            for copy in forward[t, p]:
+                copy.start()
+
+    def settle(t, p):
+        @pl.when(late)
+        def _():
+            for copy in direct[t, p]:
+                copy.wait_recv()
+
+        @pl.when(~late)
+        def _():
+            for copy in forward[t, p]:
+                copy.wait_recv()
 
     def project(t, *parts):
         return jnp.dot(
@@ -270,10 +303,12 @@
             preferred_element_type=F32,
         )
 
-    direct, forward = {}, {}
     for p in range(2):
         if p == 0:
-            near_frames(0)
+            visit(0, ((INNER, NEXT_NEAR), (INNER, NEXT_NEAR)), False)
+            for copy in partner_kv:
+                copy.wait_recv()
+            visit(0, ((PARTNER_FAR, INNER), (PARTNER_NEAR, INNER)), True)
 
             @pl.when(late)
             def _():
@@ -286,43 +321,56 @@
             def _():
                 near_frames(1)
 
+            pass_on(0, 0)
+            pass_on(1, 0)
+            for copy in w_parts:
+                copy.wait_recv()
+            w_shared = send(w_all.at[pl.ds(1, 3), rows], w_all.at[pl.ds(1, 3), rows], (partner, group))
         for copy in next_kv[NEXT_NEAR, p]:
             copy.wait_recv()
         results = [
             attend(0, p, h, NEXT_NEAR, NEXT_NEAR + 1, (top[0, p, h], acc[0, p, h])) for h in range(2)
         ]
-        direct[0, p] = finish(0, p, results)
+        finish(0, p, results)
         for h in range(2):
             now, summed = attend(1, p, h, NEXT_NEAR, NEXT_NEAR + 1, (top[1, p, h], acc[1, p, h]))
             top[1, p, h] = now
             acc[1, p, h] = summed
-        if p == 1:
-            forward[1, 0] = pass_on(1, 0, direct[1, 0])
         for copy in next_kv[NEXT_FAR, p]:
             copy.wait_recv()
         results = [
             attend(1, p, h, NEXT_FAR, NEXT_FAR + 1, (top[1, p, h], acc[1, p, h])) for h in range(2)
         ]
-        direct[1, p] = finish(1, p, results)
-        forward[0, p] = pass_on(0, p, direct[0, p])
-        if p == 0:
-            for copy in w_parts:
-                copy.wait_recv()
-            w_shared = send(w_all.at[pl.ds(1, 3), rows], w_all.at[pl.ds(1, 3), rows], (partner, group))
-
+        finish(1, p, results)
+
+    pass_on(0, 1)
     own_w.wait()
-    for copy in [w_shared] + forward[0, 0] + forward[1, 0]:
-        copy.wait_recv()
+    w_shared.wait_recv()
+    settle(0, 0)
+    settle(1, 0)
     total = project(1, (0, 0), (0, 1), (1, 0), (2, 0), (3, 0))
-    other = project(0, (0, 0), (0, 1), (1, 0), (1, 1), (2, 0), (2, 1), (3, 0))
-    for copy in forward[0, 1]:
-        copy.wait_recv()
-    mixed[inner] = (other + project(0, (3, 1))).astype(BF16)
+    other = project(0, (0, 0), (0, 1), (1, 0), (2, 0), (3, 0))
+    settle(0, 1)
+    mixed[inner] = (other + project(0, (1, 1), (2, 1), (3, 1))).astype(BF16)
     for copy in direct[1, 1]:
         copy.wait_recv()
     mixed[outer] = (total + project(1, (1, 1), (2, 1), (3, 1))).astype(BF16)
+
+    @pl.when(late)
+    def _():
+        for copy in only_late:
+            copy.wait_send()
+
+    @pl.when(~late)
+    def _():
+        for copies in forward.values():
+            for copy in copies:
+                copy.wait_send()
+
+    not_all = only_late + [copy for copies in forward.values() for copy in copies]
     for copy in sends:
-        copy.wait_send()
+        if not any(copy is other_copy for other_copy in not_all):
+            copy.wait_send()
 
 
 def body(queries, keys, values, pairs, out_weight):
@@ -335,9 +383,10 @@
     return pl.pallas_call(
         functools.partial(kernel, frames_axis, groups),
         out_shape=jax.ShapeDtypeStruct(queries.shape, BF16),
-        in_specs=[in_place] * 3 + [pl.BlockSpec(memory_space=pltpu.VMEM), in_place],
+        in_specs=[in_place] * 5,
         out_specs=pl.BlockSpec(memory_space=pltpu.VMEM),
         scratch_shapes=[
+            pltpu.VMEM(pairs.shape[::-1], jnp.int32),
             pltpu.VMEM((2, tokens, cols), BF16),
             pltpu.VMEM((2, 2, 2, tokens, 2 * PAIR), BF16),
             pltpu.VMEM((6, 2, tokens, PAIR), BF16),
@@ -347,13 +396,13 @@
             pltpu.VMEM((2, 2, 2, tokens, PAIR), F32),
             pltpu.VMEM((4, 2, 2, tokens, PAIR), BF16),
             pltpu.VMEM((4, cols, cols), BF16),
-            pltpu.SemaphoreType.DMA((35,)),
-            pltpu.SemaphoreType.DMA((35,)),
-            pltpu.SemaphoreType.DMA((10,)),
+            pltpu.SemaphoreType.DMA((40,)),
+            pltpu.SemaphoreType.DMA((40,)),
+            pltpu.SemaphoreType.DMA((11,)),
             pltpu.SemaphoreType.REGULAR,
         ],
         compiler_params=pltpu.CompilerParams(
-            collective_id=0, has_side_effects=True, vmem_limit_bytes=62 * 2**20
+            collective_id=0, has_side_effects=True, vmem_limit_bytes=GRANT
         ),
         cost_estimate=pl.CostEstimate(
             flops=2 * multiply_adds, bytes_accessed=4 * queries.size * 2, transcendentals=0

time: 38.8 us -> 36.5 us (0.941)
  the two profiles are of different devices: /device:TPU:1 before, /device:TPU:8 now
where the time goes in v3:
time: 36.5 us; the launch traced here: 36.3 us
  Pallas kernels  34.9 us (96%)
  local copies, waits for them, and re-layouts  1.43 us (4%)
    pallas_call x1, Pallas kernels, body(): pl.pallas_call(functools.partial(kernel, frames_axis, groups), out_shape=...  34.9 us
    unnamed x3, local copies, waits for them, and re-layouts  1.43 us

profile of v3, /device:TPU:8, one launch (start us, length us, event | category | flops | bytes accessed | tf_op | source)
XLA Modules:
  0.0 36.3 jit_solution(16179655939158375162)
XLA Ops:
  0.0 0.0 copy-start
  0.0 0.7 %copy-done = s32[256,2]{0,1:T(2,128)S(1)} copy-done((s32[256,2]{0,1:T(2,128)S(1)}, s32[256,2]{0,1:T(2,128)}, u32[]{:S(2)}) %copy-start) | copy-done | bytes 2072
  0.7 34.9 %shard_map.55 = bf16[2,384,256]{2,1,0:T(8,128)(2,1)S(1)} custom-call(bf16[2,384,256]{2,1,0:T(8,128)(2,1)} %q_hbm.1, bf16[2,384,256]{2,1,0:T(8,128)(2,1)} %k_hbm.1, bf16[2,384,256]{2,1,0:T(8,128)(2,1)} %v_hbm.1, s32[2,256]{1,0:T(2,128)S(1)} %bitcast.1, bf16[256,1024]{1,0:T(8,128)(2,1)} %w_hbm.1), custom_call_target="tpu_custom_call" | custom-call | flops 6442450944 | bytes 1572864 | tf_op jit(solution)/shard_map/pallas_call | solution.py:383
  35.6 0.7 %copy.7 = bf16[2,384,256]{2,1,0:T(8,128)(2,1)} copy(bf16[2,384,256]{2,1,0:T(8,128)(2,1)S(1)} %shard_map.55) | data formatting | bytes 786432
Async XLA Ops:
  0.0 0.7 %copy-start = (s32[256,2]{0,1:T(2,128)S(1)}, s32[256,2]{0,1:T(2,128)}, u32[]{:S(2)}) copy-start(s32[256,2]{0,1:T(2,128)} %param.8) | copy-start | bytes 6148

commit v4 on v3

--- a/solution.py
+++ b/solution.py
@@ -58,13 +58,15 @@
     across = lax.rem(group + 2, groups)
     outer = core
     inner = 1 - core
-    late = lax.rem(me, RUN) == 0
+    first_of_all, last_of_all = me == 0, me == frames_axis - 1
+    alone = first_of_all | last_of_all
+    late = (lax.rem(me, RUN) == 0) & ~first_of_all
 
     barrier = pltpu.get_barrier_semaphore()
     for device in ((partner, group), (me, up), (me, down), (me, across)):
         pl.semaphore_signal(barrier, inc=1, device_id=device, device_id_type=MESH)
 
-    @pl.when(core == 0)
+    @pl.when((core == 0) & ~first_of_all)
     def _():
         pl.semaphore_signal(barrier, inc=1, device_id=(beyond, group), device_id_type=MESH)
 
@@ -90,7 +92,12 @@
         9, w_hbm.at[:, pl.ds(pl.multiple_of(group * group_cols, group_cols), group_cols)], w_all.at[0]
     )
 
-    pl.semaphore_wait(barrier, 4 + core)
+    @pl.when(alone)
+    def _():
+        for frames in (k_all, v_all):
+            frames[NEXT_NEAR : NEXT_FAR + 1] = jnp.zeros((2,) + frames.shape[1:], BF16)
+
+    pl.semaphore_wait(barrier, 4 + core - last_of_all.astype(jnp.int32))
 
 
     sends = []
@@ -125,7 +132,7 @@
                 for source, target in ((k_hbm, k_all), (v_hbm, v_all))
             ]
 
-    @pl.when(core == 1)
+    @pl.when((core == 1) & ~last_of_all)
     def _():
         pl.semaphore_signal(ready, inc=1, device_id=(beyond, group), device_id_type=MESH)
         for copies in next_kv.values():
@@ -187,10 +194,9 @@
                 q_cut[t, p, h, :, 0:PAIR] = jnp.where(mine, high, nothing)
                 q_cut[t, p, h, :, PAIR : 2 * PAIR] = jnp.where(mine, low, nothing)
 
-    def attend(t, p, h, low_slot, high_slot, old):
+    def weigh(t, p, h, low_slot, high_slot, old):
         count = high_slot - low_slot
         k = k_all[low_slot:high_slot, p].reshape(count * tokens, PAIR)
-        v = v_all[low_slot:high_slot, p].reshape(count * tokens, PAIR)
         scores = lax.dot_general(
             q_cut[t, p, h], jnp.concatenate([k, k], 1), ACROSS, preferred_element_type=F32
         )
@@ -211,8 +217,12 @@
             for c in range(tokens // PAIR):
                 at = j * tokens + c * PAIR
                 weights.append(jnp.exp2((scores[:, at : at + PAIR] - less).astype(BF16)))
+        return now, jnp.concatenate(weights, 1)
+
+    def add_up(p, low_slot, high_slot, old, now, weights):
+        v = v_all[low_slot:high_slot, p].reshape((high_slot - low_slot) * tokens, PAIR)
         summed = jnp.dot(
-            jnp.concatenate(weights, 1),
+            weights,
             jnp.concatenate([v, jnp.ones_like(v)], 1),
             preferred_element_type=F32,
         )
@@ -227,12 +237,22 @@
             for copy in copies:
                 copy.start()
 
-    @pl.when((core == 0) & ~late)
+    @pl.when((core == 0) & ~late & ~first_of_all)
     def _():
         start_beyond()
 
     for copy in own_kv:
         copy.wait()
+
+    def attend(t, p, h, low_slot, high_slot, old):
+        return add_up(p, low_slot, high_slot, old, *weigh(t, p, h, low_slot, high_slot, old))
+
+    def attend_beyond(t, p, slot):
+        olds = [(top[t, p, h], acc[t, p, h]) for h in range(2)]
+        weighed = [weigh(t, p, h, slot, slot + 1, olds[h]) for h in range(2)]
+        if t == slot - NEXT_NEAR:
+            pl.when(~alone)(next_kv[slot, p][1].wait_recv)
+        return [add_up(p, slot, slot + 1, old, *pair) for old, pair in zip(olds, weighed)]
 
     def visit(p, reach, merge):
         for t, (low_slot, high_slot) in enumerate(reach):
@@ -326,22 +346,13 @@
             for copy in w_parts:
                 copy.wait_recv()
             w_shared = send(w_all.at[pl.ds(1, 3), rows], w_all.at[pl.ds(1, 3), rows], (partner, group))
-        for copy in next_kv[NEXT_NEAR, p]:
-            copy.wait_recv()
-        results = [
-            attend(0, p, h, NEXT_NEAR, NEXT_NEAR + 1, (top[0, p, h], acc[0, p, h])) for h in range(2)
-        ]
-        finish(0, p, results)
-        for h in range(2):
-            now, summed = attend(1, p, h, NEXT_NEAR, NEXT_NEAR + 1, (top[1, p, h], acc[1, p, h]))
+        pl.when(~alone)(next_kv[NEXT_NEAR, p][0].wait_recv)
+        finish(0, p, attend_beyond(0, p, NEXT_NEAR))
+        for h, (now, summed) in enumerate(attend_beyond(1, p, NEXT_NEAR)):
             top[1, p, h] = now
             acc[1, p, h] = summed
-        for copy in next_kv[NEXT_FAR, p]:
-            copy.wait_recv()
-        results = [
-            attend(1, p, h, NEXT_FAR, NEXT_FAR + 1, (top[1, p, h], acc[1, p, h])) for h in range(2)
-        ]
-        finish(1, p, results)
+        pl.when(~alone)(next_kv[NEXT_FAR, p][0].wait_recv)
+        finish(1, p, attend_beyond(1, p, NEXT_FAR))
 
     pass_on(0, 1)
     own_w.wait()
@@ -367,7 +378,13 @@
             for copy in copies:
                 copy.wait_send()
 
-    not_all = only_late + [copy for copies in forward.values() for copy in copies]
+    @pl.when(~alone)
+    def _():
+        for copies in next_kv.values():
+            for copy in copies:
+                copy.wait_send()
+
+    not_all = only_late + [copy for copies in next_kv.values() for copy in copies] + [copy for copies in forward.values() for copy in copies]
     for copy in sends:
         if not any(copy is other_copy for other_copy in not_all):
             copy.wait_send()

time: 36.5 us -> 34.9 us (0.956)
  the two profiles are of different devices: /device:TPU:8 before, /device:TPU:1 now
where the time goes in v4:
time: 34.9 us; the launch traced here: 34.7 us
  Pallas kernels  33.3 us (95%)
  local copies, waits for them, and re-layouts  1.43 us (4%)
    pallas_call x1, Pallas kernels, body(): pl.pallas_call(functools.partial(kernel, frames_axis, groups), out_shape=...  33.3 us
    unnamed x3, local copies, waits for them, and re-layouts  1.43 us

profile of v4, /device:TPU:1, one launch (start us, length us, event | category | flops | bytes accessed | tf_op | source)
XLA Modules:
  0.0 34.7 jit_solution(11266497740977563038)
XLA Ops:
  0.0 0.0 copy-start
  0.0 0.7 %copy-done = s32[256,2]{0,1:T(2,128)S(1)} copy-done((s32[256,2]{0,1:T(2,128)S(1)}, s32[256,2]{0,1:T(2,128)}, u32[]{:S(2)}) %copy-start) | copy-done | bytes 2072
  0.7 33.3 %shard_map.55 = bf16[2,384,256]{2,1,0:T(8,128)(2,1)S(1)} custom-call(bf16[2,384,256]{2,1,0:T(8,128)(2,1)} %q_hbm.1, bf16[2,384,256]{2,1,0:T(8,128)(2,1)} %k_hbm.1, bf16[2,384,256]{2,1,0:T(8,128)(2,1)} %v_hbm.1, s32[2,256]{1,0:T(2,128)S(1)} %bitcast.1, bf16[256,1024]{1,0:T(8,128)(2,1)} %w_hbm.1), custom_call_target="tpu_custom_call" | custom-call | flops 6442450944 | bytes 1572864 | tf_op jit(solution)/shard_map/pallas_call | solution.py:400
  34.0 0.7 %copy.7 = bf16[2,384,256]{2,1,0:T(8,128)(2,1)} copy(bf16[2,384,256]{2,1,0:T(8,128)(2,1)S(1)} %shard_map.55) | data formatting | bytes 786432
Async XLA Ops:
  0.0 0.7 %copy-start = (s32[256,2]{0,1:T(2,128)S(1)}, s32[256,2]{0,1:T(2,128)}, u32[]{:S(2)}) copy-start(s32[256,2]{0,1:T(2,128)} %param.8) | copy-start | bytes 6148

commit v5 on v4

--- a/solution.py
+++ b/solution.py
@@ -270,17 +270,16 @@
     def finish(t, p, results):
         parts = [summed[:, 0:PAIR] / summed[:, PAIR : 2 * PAIR] for _, summed in results]
         gathered[0, t, p] = jnp.where(first, parts[0], parts[1]).astype(BF16)
-        direct[t, p] = [
-            send(gathered.at[0, t, p], gathered.at[place, t, p], (me, there))
-            for place, there in ((1, up), (2, down))
-        ]
         whole = prepare(gathered.at[0, t, p], gathered.at[3, t, p], (me, across))
         if (t, p) == (1, 1):
             whole.start()
         else:
             pl.when(late)(whole.start)
             only_late.append(whole)
-        direct[t, p].append(whole)
+        direct[t, p] = [
+            send(gathered.at[0, t, p], gathered.at[place, t, p], (me, there))
+            for place, there in ((1, up), (2, down))
+        ] + [whole]
 
     half = tokens // 2
 

time: 34.9 us -> 34.6 us (level)
  Pallas kernels: 33.3 us -> 32.9 us
    pallas_call x1, Pallas kernels: 33.3 us -> 32.9 us  [body(): pl.pallas_call(functools.partial(kernel, frames_axis, groups), out_shape=...]
where the time goes in v5:
time: 34.6 us; the launch traced here: 34.3 us
  Pallas kernels  32.9 us (95%)
  local copies, waits for them, and re-layouts  1.43 us (4%)
    pallas_call x1, Pallas kernels, body(): pl.pallas_call(functools.partial(kernel, frames_axis, groups), out_shape=...  32.9 us
    unnamed x3, local copies, waits for them, and re-layouts  1.43 us

profile of v5, /device:TPU:1, one launch (start us, length us, event | category | flops | bytes accessed | tf_op | source)
XLA Modules:
  0.0 34.3 jit_solution(8887465333742786818)
XLA Ops:
  0.0 0.0 copy-start
  0.0 0.7 %copy-done = s32[256,2]{0,1:T(2,128)S(1)} copy-done((s32[256,2]{0,1:T(2,128)S(1)}, s32[256,2]{0,1:T(2,128)}, u32[]{:S(2)}) %copy-start) | copy-done | bytes 2072
  0.7 32.9 %shard_map.55 = bf16[2,384,256]{2,1,0:T(8,128)(2,1)S(1)} custom-call(bf16[2,384,256]{2,1,0:T(8,128)(2,1)} %q_hbm.1, bf16[2,384,256]{2,1,0:T(8,128)(2,1)} %k_hbm.1, bf16[2,384,256]{2,1,0:T(8,128)(2,1)} %v_hbm.1, s32[2,256]{1,0:T(2,128)S(1)} %bitcast.1, bf16[256,1024]{1,0:T(8,128)(2,1)} %w_hbm.1), custom_call_target="tpu_custom_call" | custom-call | flops 6442450944 | bytes 1572864 | tf_op jit(solution)/shard_map/pallas_call | solution.py:399
  33.6 0.7 %copy.7 = bf16[2,384,256]{2,1,0:T(8,128)(2,1)} copy(bf16[2,384,256]{2,1,0:T(8,128)(2,1)S(1)} %shard_map.55) | data formatting | bytes 786432
Async XLA Ops:
  0.0 0.7 %copy-start = (s32[256,2]{0,1:T(2,128)S(1)}, s32[256,2]{0,1:T(2,128)}, u32[]{:S(2)}) copy-start(s32[256,2]{0,1:T(2,128)} %param.8) | copy-start | bytes 6148
